TPU v7x, 32 devices: a whole 2x2x4 slice. The times are simulated.
32 devices in a mesh: groups: 2 (over x), fsdp: 4 (over y, core), tp: 4 (over z).
Axes of the slice: x: 2, y: 2, z: 4, core: 2. Of those that a mesh axis runs over, the one named last changes fastest.
Arguments:
- hidden: bfloat16 [64, 4, 8192], P(('groups', 'fsdp')), parts along dimension 0, may hold values from -6 to 6
- queries: bfloat16 [64, 4, 8192], P(('groups', 'fsdp'), None, 'tp'), parts along dimension 0, may hold values from -6 to 6
- key_value_weight: bfloat16 [2, 8192, 1024], P(None, None, 'tp'), may hold values from -0.0625 to 0.0625
- adapter_down_weight: bfloat16 [4, 64, 8192], P('groups', None, ('fsdp', 'tp')), parts along dimension 0, may hold values from -0.0625 to 0.0625
- adapter_up_weight: bfloat16 [4, 1024, 64], P('groups', 'tp', 'fsdp'), parts along dimension 0, may hold values from -0.5 to 0.5
- rotated_cache_states: bfloat16 [2, 64, 8, 1536, 128], P(None, ('groups', 'fsdp'), 'tp'), parts along dimension 1, may hold values from -6 to 6
- cache_fill_length: int32 [64], P(('groups', 'fsdp')), parts along dimension 0, may hold values from 1 to 1536, as said below
Outputs:
- new_kv: bfloat16 [2, 64, 4, 1024], P(None, ('groups', 'fsdp'), None, 'tp'), parts along dimension 1
- attended: bfloat16 [64, 4, 8192], P(('groups', 'fsdp'), None, 'tp'), parts along dimension 0
There are 2 independent parts, one for each index of `groups`. A program takes and returns all parts, laid end to end along the dimension named above; an argument that names none is the same for every part. Nothing has to cross between parts.
Inputs may be any that keep to these rules, and one draw needn't show every extreme that they name: `cache_fill_length`: the first row has exactly 1536 filled slots.
All inputs are finite; a program needn't handle non-finite values.
Results may differ from a plain program's by a relative error of at most 0.0071.
Values may be sent and summed in bfloat16 or wider, within the bound.
A program may use at most 128 MiB of HBM per device.

v0:
```python
import jax
import jax.numpy as jnp
from jax import lax
from jax.sharding import PartitionSpec as P

adapter_scale = 2.0
rope_theta = 500000.0


def rotate(values, position):
    half_dim = values.shape[-1] // 2
    freqs = rope_theta ** (-2.0 * jnp.arange(half_dim, dtype=jnp.float32) / values.shape[-1])
    angles = position[:, :, None, None] * freqs
    cosine = jnp.cos(angles)
    sine = jnp.sin(angles)
    first = values[..., :half_dim]
    second = values[..., half_dim:]
    return jnp.concatenate(
        [first * cosine - second * sine, second * cosine + first * sine], axis=-1
    )


def cache_part(qrot, rotated_cache_states, cache_fill_length):
    head_dim = qrot.shape[-1]
    scores = jnp.einsum(
        "rskgd,rkld->rkgsl", qrot, rotated_cache_states[0], preferred_element_type=jnp.float32
    )
    scores = scores / jnp.sqrt(jnp.float32(head_dim))
    slot_live = (
        jnp.arange(rotated_cache_states.shape[3], dtype=jnp.int32)[None, :]
        < cache_fill_length[:, None]
    )
    return jnp.where(slot_live[:, None, None, None, :], scores, -jnp.inf)


def on_device(
    hidden,
    queries,
    key_value_weight,
    adapter_down_weight,
    adapter_up_weight,
    rotated_cache_states,
    cache_fill_length,
):
    rows_here = hidden.shape[0]
    steps = hidden.shape[1]
    head_dim = rotated_cache_states.shape[4]
    kv_here = rotated_cache_states.shape[2]
    group = queries.shape[2] // (kv_here * head_dim)
    position = (cache_fill_length[:, None] + jnp.arange(steps, dtype=jnp.int32)[None, :]).astype(
        jnp.float32
    )
    qrot = rotate(
        queries.astype(jnp.float32).reshape(rows_here, steps, kv_here * group, head_dim), position
    ).astype(jnp.bfloat16)
    qrot = qrot.reshape(rows_here, steps, kv_here, group, head_dim)
    up_factor_columns = lax.all_gather(adapter_up_weight, "fsdp", axis=2, tiled=True)
    adapter_update = jnp.einsum(
        "zrd,zcr->zdc",
        lax.all_gather(adapter_down_weight, ("fsdp", "tp"), axis=2, tiled=True),
        up_factor_columns,
        preferred_element_type=jnp.float32,
    )
    merged_weight = key_value_weight.astype(jnp.float32) + adapter_scale * adapter_update
    projected_output = jnp.einsum(
        "rsd,zdc->zrsc", hidden.astype(jnp.float32), merged_weight, precision=lax.Precision.HIGHEST
    )
    cache_scores = cache_part(qrot, rotated_cache_states, cache_fill_length)
    keys_new = rotate(
        projected_output[0].reshape(rows_here, steps, kv_here, head_dim), position
    ).astype(jnp.bfloat16)
    values_new = (
        projected_output[1].reshape(rows_here, steps, kv_here, head_dim).astype(jnp.bfloat16)
    )
    new_kv = jnp.stack(
        [
            keys_new.reshape(rows_here, steps, kv_here * head_dim),
            values_new.reshape(rows_here, steps, kv_here * head_dim),
        ]
    )
    new_scores = jnp.einsum("rskgd,rtkd->rkgst", qrot, keys_new, preferred_element_type=jnp.float32)
    new_scores = new_scores / jnp.sqrt(jnp.float32(head_dim))
    causal = jnp.arange(steps)[None, :] <= jnp.arange(steps)[:, None]
    new_scores = jnp.where(causal[None, None, None, :, :], new_scores, -jnp.inf)
    peak = jnp.maximum(
        jnp.max(cache_scores, axis=-1, keepdims=True), jnp.max(new_scores, axis=-1, keepdims=True)
    )
    cache_expo = jnp.exp(cache_scores - peak)
    new_expo = jnp.exp(new_scores - peak)
    totals = jnp.sum(cache_expo, axis=-1, keepdims=True) + jnp.sum(new_expo, axis=-1, keepdims=True)
    cache_weights = (cache_expo / totals).astype(jnp.bfloat16)
    new_weights = (new_expo / totals).astype(jnp.bfloat16)
    output = jnp.einsum(
        "rkgsl,rkld->rskgd",
        cache_weights,
        rotated_cache_states[1],
        preferred_element_type=jnp.float32,
    )
    output = output + jnp.einsum(
        "rkgst,rtkd->rskgd", new_weights, values_new, preferred_element_type=jnp.float32
    )
    attended = output.reshape(rows_here, steps, kv_here * group * head_dim).astype(jnp.bfloat16)
    return (new_kv, attended)


def solution(mesh):
    return jax.shard_map(
        on_device,
        mesh=mesh,
        in_specs=(
            P(("groups", "fsdp"), None, None),
            P(("groups", "fsdp"), None, "tp"),
            P(None, None, "tp"),
            P("groups", None, ("fsdp", "tp")),
            P("groups", "tp", "fsdp"),
            P(None, ("groups", "fsdp"), "tp", None, None),
            P(("groups", "fsdp")),
        ),
        out_specs=(P(None, ("groups", "fsdp"), None, "tp"), P(("groups", "fsdp"), None, "tp")),
        check_vma=False,
    )
```

profile of v0, /device:TPU:0, one launch (start us, length us, event | category | flops | bytes accessed | tf_op | source)
XLA Modules:
  0.0 90.6 jit_solution(2426760279746896611)
XLA Ops:
  7.2 0.0 all-gather.2.cloned.1.call-start
  7.2 0.7 all-gather.2.cloned.1.call-update
  7.9 1.0 %reshape.108 = f32[8,4,16,128]{3,2,1,0:T(8,128)S(1)} reshape(bf16[8,4,2048]{2,1,0:T(4,128)(2,1)} %param.8) | data formatting | bytes 393216 | tf_op jit(solution)/shard_map/reshape | solution.py:54
  8.9 6.5 %all_gather.7 = bf16[2,256,64]{1,2,0:T(8,128)(2,1)S(1)} all-gather(bf16[2,256,16]{1,2,0:T(8,128)(2,1)} %param.11), channel_id=1, replica_groups=mesh['groups'=2,'fsdp'=4,'tp'=4] {'fsdp'}, dimensions={2}, use_global_device_ids=true | all-gather | bytes 81920 | tf_op jit(solution)/shard_map/all_gather | solution.py:57
  15.3 0.5 iota_compare_fusion.1
  15.9 0.7 add_convert_fusion.1
  16.6 0.2 multiply_cosine_fusion
  16.8 0.2 fusion.34
  17.0 0.7 iota_compare_fusion
  17.7 5.2 %bitcast_reduce_fusion = (f32[8,2,8,4]{2,3,1,0:T(4,128)S(1)}, f32[8,2,4,8,1536]{4,3,2,1,0:T(8,128)S(1)}) fusion(bf16[2,8,2,1536,128]{4,3,2,1,0:T(8,128)(2,1)} %param.12, pred[8,1536]{1,0:T(8,128)(4,1)S(1)} %iota_compare_fusion, bf16[8,4,2,8,64]{4,3,2,1,0:T(8,128)(2,1)S(1)} %get-tuple-element.7, bf16[8,4,2,8,64]{4,3,2,1,0:T(8,128)(2,1)S(1)} %get-tuple-element.6), kind=kOutput, calls=%fused_computation.14 | convolution fusion | flops 203947520 | bytes 9582592 | tf_op jit(solution)/shard_map/rskgd,rkld->rkgsl/dot_general | solution.py:25
  22.9 31.1 %all-gather.2.cloned.1.call-done = bf16[2,64,8192]{2,1,0:T(8,128)(2,1)} async-done(((bf16[2,64,512]{2,1,0:T(8,128)(2,1)}), bf16[2,64,8192]{2,1,0:T(8,128)(2,1)}) %all-gather.2.cloned.1.call-update) | async-done | bytes 2097168 | tf_op jit(solution)/shard_map/all_gather | solution.py:60
  54.0 0.0 copy-start
  54.0 9.7 %fusion.46 = f32[2,8192,256]{2,1,0:T(8,128)} fusion(bf16[2,64,8192]{2,1,0:T(8,128)(2,1)} %all-gather.2.cloned.1.call-done, bf16[2,256,64]{1,2,0:T(8,128)(2,1)S(1)} %all_gather.7), kind=kOutput, calls=%fused_computation.62 | convolution fusion | flops 536870912 | bytes 18939904 | tf_op jit(solution)/shard_map/zrd,zcr->zdc/dot_general | solution.py:58
  63.7 0.0 copy-done
  63.8 0.0 copy-start.1
  63.8 12.6 %fusion.29 = f32[2,8,4,256]{3,1,2,0:T(8,128)S(1)} fusion(f32[2,8192,256]{2,1,0:T(8,128)} %fusion.46, bf16[2,8192,256]{2,1,0:T(8,128)(2,1)} %param.9, bf16[8,4,8192]{2,1,0:T(4,128)(2,1)S(1)} %copy-done), kind=kOutput, calls=%fused_computation.28 | convolution fusion | flops 1623195648 | bytes 25755648 | tf_op jit(solution)/shard_map/rsd,zdc->zrsc/dot_general | solution.py:65
  76.4 0.1 fusion.44
  76.5 0.1 maximum_convert_fusion
  76.6 0.0 copy-done.1
  76.6 0.8 fusion.45
  77.4 0.1 fusion.38
  77.5 0.6 fusion.19
  78.2 4.0 %fusion.22 = f32[8,4,2,8,128]{4,3,1,2,0:T(8,128)S(1)} fusion(bf16[2,8,2,1536,128]{4,3,2,1,0:T(8,128)(2,1)} %param.12, f32[8,2,4,8,1536]{4,3,2,1,0:T(8,128)S(1)} %get-tuple-element.15, f32[8,2,8,4]{2,3,1,0:T(4,128)S(1)} %add.43, f32[8,2,8,4]{2,3,1,0:T(4,128)S(1)} %max.8), kind=kOutput, calls=%fused_computation.21 | convolution fusion | flops 203685888 | bytes 9703424 | tf_op jit(solution)/shard_map/rkgsl,rkld->rskgd/dot_general | solution.py:93
  82.1 0.3 fusion.26
  82.4 0.7 reshape.115
  83.1 0.6 copy.23
  (10 shorter events, 0.1 us)
Async XLA Ops:
  7.2 46.8 %all-gather.2.cloned.1.call-start = ((), (), s32[]{:S(2)}) async-start(), calls=%async_computation | async-start | bytes 2228224 | tf_op jit(solution)/shard_map/all_gather | solution.py:60
  54.0 9.8 %copy-start = (bf16[8,4,8192]{2,1,0:T(4,128)(2,1)S(1)}, bf16[8,4,8192]{2,1,0:T(4,128)(2,1)}, u32[]{:S(2)}) copy-start(bf16[8,4,8192]{2,1,0:T(4,128)(2,1)} %param.7) | copy-start | bytes 1572868
  63.8 12.9 %copy-start.1 = (pred[4,4]{1,0:T(4,128)(4,1)S(1)}, pred[4,4]{1,0:T(4,128)(4,1)}, u32[]{:S(2)}) copy-start(pred[4,4]{1,0:T(4,128)(4,1)} %iota_compare_fusion.1) | copy-start | bytes 52
Sparse Core Ops, SparseCore 0:
  10.1 43.8 all-gather.1
where the time goes:
time: 90.9 us; the launch traced here: 90.6 us
  matrix products  32.5 us (36%)
  waiting for transfers between devices  31.8 us (35%)
  between operations  14.2 us (16%)
  blocking collectives  6.46 us (7%)
  other arithmetic  3.25 us (4%)
  local copies, waits for them, and re-layouts  2.42 us (3%)
    all_gather x1, waiting for transfers between devices, on_device(): lax.all_gather(adapter_down_weight, ('fsdp', 'tp'), axis=2, tiled=True)  31.1 us
    dot_general x1, matrix products, on_device(): jnp.einsum('rsd,zdc->zrsc', hidden.astype(jnp.float32), merged_weight, pr...  12.6 us
    dot_general x1, matrix products, on_device(): jnp.einsum('zrd,zcr->zdc', lax.all_gather(adapter_down_weight, ('fsdp', '...  9.75 us
    all_gather x1, blocking collectives, on_device(): lax.all_gather(adapter_up_weight, 'fsdp', axis=2, tiled=True)  6.46 us
    dot_general x1, matrix products, cache_part(): jnp.einsum('rskgd,rkld->rkgsl', qrot, rotated_cache_states[0], preferred_...  5.18 us
    dot_general x1, matrix products, on_device(): jnp.einsum('rkgsl,rkld->rskgd', cache_weights, rotated_cache_states[1], p...  3.95 us
  transfers between devices with their start and end apart: 1, of which 1 were waited for; matrix products, arithmetic and copies ran while one was open for 9% of the time, Pallas kernels for 0%

commit v1 on v0

--- a/solution.py
+++ b/solution.py
@@ -1,6 +1,12 @@
+import functools
+import math
+
 import jax
 import jax.numpy as jnp
+import numpy as np
 from jax import lax
+from jax.experimental import pallas as pl
+from jax.experimental.pallas import tpu as pltpu
 from jax.sharding import PartitionSpec as P
 
 adapter_scale = 2.0
@@ -33,7 +39,7 @@
     return jnp.where(slot_live[:, None, None, None, :], scores, -jnp.inf)
 
 
-def on_device(
+def on_device_plain(
     hidden,
     queries,
     key_value_weight,
@@ -102,10 +108,366 @@
     attended = output.reshape(rows_here, steps, kv_here * group * head_dim).astype(jnp.bfloat16)
     return (new_kv, attended)
 
+MESH = pl.DeviceIdType.MESH
+W_CHUNKS = 4
+NT = (((1,), (1,)), ((), ()))
+
+
+def dot_nt(a, b):
+    return lax.dot_general(a, b, NT, preferred_element_type=jnp.float32)
+
+
+def dot_nn(a, b):
+    return jnp.dot(a, b, preferred_element_type=jnp.float32)
+
+
+def kernel(
+    fill_ref,
+    freq_ref,
+    hidden_hbm,
+    queries_hbm,
+    weight_hbm,
+    down_hbm,
+    up_ref,
+    cache_hbm,
+    new_kv_ref,
+    attended_ref,
+    hidden_raw,
+    hidden_flat,
+    queries_raw,
+    weight,
+    down,
+    up_t,
+    low,
+    keys,
+    values,
+    cos_q,
+    sin_q,
+    q_rot,
+    out_acc,
+    peak_acc,
+    sum_acc,
+    in_sem,
+    weight_sem,
+    key_sem,
+    value_sem,
+    down_send,
+    down_recv,
+    up_send,
+    up_recv,
+    low_send,
+    low_recv,
+):
+    rows, steps, width = hidden_raw.shape
+    tokens = rows * steps
+    kv_here, slots, head_dim = keys.shape[1], keys.shape[2], keys.shape[3]
+    half = head_dim // 2
+    group = queries_raw.shape[2] // (kv_here * head_dim)
+    per_row = group * steps
+    part = down.shape[-1]
+    rank_here = up_ref.shape[2]
+    tp = low.shape[0]
+    f = lax.axis_index("fsdp")
+    t = lax.axis_index("tp")
+    sibling = f + 1 - 2 * lax.rem(f, 2)
+    across = lax.rem(f + 2, 4)
+    diagonal = sibling + 2 - 4 * (sibling // 2)
+    owners = (f, sibling, across, diagonal)
+
+    hidden_copy = pltpu.make_async_copy(hidden_hbm, hidden_raw, in_sem.at[0])
+    hidden_copy.start()
+    queries_copy = pltpu.make_async_copy(queries_hbm, queries_raw, in_sem.at[1])
+    queries_copy.start()
+    down_copy = pltpu.make_async_copy(down_hbm, down.at[0], in_sem.at[2])
+    down_copy.start()
+    depth = width // W_CHUNKS
+    weight_copies = []
+    for c in range(W_CHUNKS):
+        for z in range(2):
+            span = pl.ds(c * depth, depth)
+            copy = pltpu.make_async_copy(
+                weight_hbm.at[z, span], weight.at[z, span], weight_sem.at[z, c]
+            )
+            copy.start()
+            weight_copies.append(copy)
+
+    @pl.loop(0, rows)
+    def _(r):
+        pltpu.make_async_copy(cache_hbm.at[0, r], keys.at[r], key_sem.at[r]).start()
+        pltpu.make_async_copy(cache_hbm.at[1, r], values.at[r], value_sem.at[r]).start()
+
+    barrier = pltpu.get_barrier_semaphore()
+    for peer in owners[1:]:
+        pl.semaphore_signal(barrier, inc=1, device_id={"fsdp": peer}, device_id_type=MESH)
+    for d in range(1, tp):
+        pl.semaphore_signal(
+            barrier, inc=1, device_id={"tp": lax.rem(t + d, tp)}, device_id_type=MESH
+        )
+    pl.semaphore_wait(barrier, 3 + tp - 1)
+
+    def send_down(source, slot, z, peer, sem):
+        return pltpu.make_async_remote_copy(
+            src_ref=source.at[z],
+            dst_ref=down.at[slot, z],
+            send_sem=down_send.at[sem, z],
+            recv_sem=down_recv.at[sem, z],
+            device_id={"fsdp": peer},
+            device_id_type=MESH,
+        )
+
+    to_across = [send_down(down_hbm, 2, z, across, 1) for z in range(2)]
+    to_sibling = [send_down(down_hbm, 1, z, sibling, 0) for z in range(2)]
+    forward = [send_down(down.at[2], 3, z, sibling, 2) for z in range(2)]
+    for copy in to_across + to_sibling:
+        copy.start()
+
+    mine = pl.ds(pl.multiple_of(f * rank_here, rank_here), rank_here)
+    eye = (
+        lax.broadcasted_iota(jnp.int32, (rank_here, rank_here), 0)
+        == lax.broadcasted_iota(jnp.int32, (rank_here, rank_here), 1)
+    ).astype(jnp.float32).astype(jnp.bfloat16)
+    for z in range(2):
+        up_t[z, mine, :] = dot_nt(eye, up_ref[z]).astype(jnp.bfloat16)
+    up_copies = []
+    for n, peer in enumerate(owners[1:]):
+        copy = pltpu.make_async_remote_copy(
+            src_ref=up_t.at[:, mine, :],
+            dst_ref=up_t.at[:, mine, :],
+            send_sem=up_send.at[n],
+            recv_sem=up_recv.at[n],
+            device_id={"fsdp": peer},
+            device_id_type=MESH,
+        )
+        copy.start()
+        up_copies.append(copy)
+
+    lane = lax.broadcasted_iota(jnp.int32, (1, head_dim), 1)
+    sign = jnp.where(lane < half, -1.0, 1.0).astype(jnp.float32)
+    freq = freq_ref[...]
+
+    def tables(count, each):
+        at = lax.broadcasted_iota(jnp.int32, (count, head_dim), 0)
+        position = lax.rem(at, steps)
+        for r in range(rows):
+            position = position + jnp.where(at // each == r, fill_ref[r], 0)
+        angle = position.astype(jnp.float32) * freq
+        return jnp.cos(angle), jnp.sin(angle) * sign
+
+    cos_all, sin_all = tables(rows * 2 * steps, 2 * steps)
+    cos_q[...] = cos_all
+    sin_q[...] = sin_all
+    cos_k, sin_k = tables(tokens, steps)
+
+    hidden_copy.wait()
+    block = 512
+    for c in range(width // block):
+        span = slice(c * block, (c + 1) * block)
+        hidden_flat[:, span] = (
+            hidden_raw[:, :, span].astype(jnp.float32).reshape(tokens, block).astype(jnp.bfloat16)
+        )
+
+    base = [jnp.zeros((tokens, weight.shape[2]), jnp.float32) for _ in range(2)]
+    for c in range(W_CHUNKS):
+        for z in range(2):
+            weight_copies[c * 2 + z].wait()
+            span = slice(c * depth, (c + 1) * depth)
+            base[z] = base[z] + dot_nn(hidden_flat[:, span], weight[z, span, :])
+
+    def low_of(slot):
+        span = pl.ds(pl.multiple_of((owners[slot] * tp + t) * part, part), part)
+        factors = down[slot].reshape(down.shape[1] * down.shape[2], part)
+        return dot_nt(hidden_flat[:, span], factors)
+
+    down_copy.wait()
+    partial = low_of(0)
+    for z in range(2):
+        to_sibling[z].wait_recv()
+    partial = partial + low_of(1)
+    for z in range(2):
+        to_across[z].wait_recv()
+        forward[z].start()
+    partial = partial + low_of(2)
+    for z in range(2):
+        forward[z].wait_recv()
+    partial = partial + low_of(3)
+    low[t] = partial
+    low_copies = []
+    for d in range(1, tp):
+        copy = pltpu.make_async_remote_copy(
+            src_ref=low.at[t],
+            dst_ref=low.at[t],
+            send_sem=low_send.at[d - 1],
+            recv_sem=low_recv.at[d - 1],
+            device_id={"tp": lax.rem(t + d, tp)},
+            device_id_type=MESH,
+        )
+        copy.start()
+        low_copies.append(copy)
+
+    queries_copy.wait()
+    factor = math.log2(math.e) / math.sqrt(head_dim)
+    slot_at = lax.broadcasted_iota(jnp.int32, (per_row, slots), 1)
+
+    @pl.loop(0, rows)
+    def _(r):
+        table = pl.ds(pl.multiple_of(r * 2 * steps, 2 * steps), 2 * steps)
+        cosine = jnp.concatenate([cos_q[table, :]] * (group // 2), axis=0)
+        sine = jnp.concatenate([sin_q[table, :]] * (group // 2), axis=0)
+        here = pl.ds(pl.multiple_of(r * per_row, per_row), per_row)
+        row = queries_raw[r].astype(jnp.float32)
+        live = slot_at < fill_ref[r]
+        pltpu.make_async_copy(cache_hbm.at[0, r], keys.at[r], key_sem.at[r]).wait()
+        pltpu.make_async_copy(cache_hbm.at[1, r], values.at[r], value_sem.at[r]).wait()
+        for k in range(kv_here):
+            first = k * group
+            q = jnp.concatenate(
+                [row[:, (first + g) * head_dim : (first + g + 1) * head_dim] for g in range(group)],
+                axis=0,
+            )
+            q = (q * cosine + pltpu.roll(q, half, 1) * sine).astype(jnp.bfloat16)
+            q_rot[k, here, :] = q
+            scores = jnp.where(live, dot_nt(q, keys[r, k]), -1e30)
+            peak = jnp.max(scores, axis=1, keepdims=True)
+            expo = jnp.exp2((scores - peak) * factor)
+            out_acc[k, here, :] = dot_nn(expo.astype(jnp.bfloat16), values[r, k])
+            peak_acc[k, here, :] = jnp.broadcast_to(peak, (per_row, head_dim))
+            total = jnp.sum(expo, axis=1, keepdims=True)
+            sum_acc[k, here, :] = jnp.broadcast_to(total, (per_row, head_dim))
+
+    for copy in low_copies:
+        copy.wait_recv()
+    for copy in up_copies:
+        copy.wait_recv()
+    low_all = low[0]
+    for d in range(1, tp):
+        low_all = low_all + low[d]
+    ranks = up_t.shape[1]
+    proj = []
+    for z in range(2):
+        low_z = low_all[:, z * ranks : (z + 1) * ranks]
+        high = low_z.astype(jnp.bfloat16)
+        rest = (low_z - high.astype(jnp.float32)).astype(jnp.bfloat16)
+        factors = up_t[z]
+        update = dot_nn(high, factors) + dot_nn(rest, factors)
+        proj.append(base[z] + adapter_scale * update)
+    count = rows * per_row
+    row_at = lax.broadcasted_iota(jnp.int32, (count, tokens), 0)
+    col_at = lax.broadcasted_iota(jnp.int32, (count, tokens), 1)
+    seen = (row_at // per_row == col_at // steps) & (
+        lax.rem(col_at, steps) <= lax.rem(row_at, steps)
+    )
+    for k in range(kv_here):
+        columns = slice(k * head_dim, (k + 1) * head_dim)
+        key = proj[0][:, columns]
+        key = key * cos_k + pltpu.roll(key, half, 1) * sin_k
+        value = proj[1][:, columns]
+        for r in range(rows):
+            span = slice(r * steps, (r + 1) * steps)
+            new_kv_ref[0, r, :, columns] = key[span].astype(jnp.bfloat16)
+            new_kv_ref[1, r, :, columns] = value[span].astype(jnp.bfloat16)
+        scores = jnp.where(seen, dot_nt(q_rot[k], key.astype(jnp.bfloat16)), -1e30)
+        peak_old = peak_acc[k]
+        peak = jnp.maximum(peak_old, jnp.max(scores, axis=1, keepdims=True))
+        expo = jnp.exp2((scores - peak[:, :tokens]) * factor)
+        keep = jnp.exp2((peak_old - peak) * factor)
+        total = sum_acc[k] * keep + jnp.sum(expo, axis=1, keepdims=True)
+        output = out_acc[k] * keep + dot_nn(expo.astype(jnp.bfloat16), value.astype(jnp.bfloat16))
+        output = output / total
+        for r in range(rows):
+            for g in range(group):
+                at = r * per_row + g * steps
+                head = k * group + g
+                attended_ref[r, :, head * head_dim : (head + 1) * head_dim] = output[
+                    at : at + steps
+                ].astype(jnp.bfloat16)
+
+    for copy in to_across + to_sibling + forward + up_copies + low_copies:
+        copy.wait_send()
+
+
+def on_device_kernel(hidden, queries, weight, down, up, cache, fill, tp):
+    rows, steps, _ = hidden.shape
+    tokens = rows * steps
+    kv_here, head_dim = cache.shape[2], cache.shape[4]
+    per_row = queries.shape[2] // (kv_here * head_dim) * steps
+    freqs = rope_theta ** (-2.0 * (np.arange(head_dim) % (head_dim // 2)) / head_dim)
+    freqs = jnp.asarray(freqs[None, :], jnp.float32)
+    any_spec = pl.BlockSpec(memory_space=pl.ANY)
+    vmem_spec = pl.BlockSpec(memory_space=pltpu.VMEM)
+    dma = pltpu.SemaphoreType.DMA
+    f32, bf16 = jnp.float32, jnp.bfloat16
+    moved = sum(math.prod(a.shape) * 2 for a in (hidden, weight, cache))
+    return pl.pallas_call(
+        kernel,
+        out_shape=(
+            jax.ShapeDtypeStruct((2, rows, steps, weight.shape[2]), bf16),
+            jax.ShapeDtypeStruct(queries.shape, bf16),
+        ),
+        in_specs=[
+            pl.BlockSpec(memory_space=pltpu.SMEM),
+            vmem_spec,
+            any_spec,
+            any_spec,
+            any_spec,
+            any_spec,
+            vmem_spec,
+            any_spec,
+        ],
+        out_specs=(vmem_spec, vmem_spec),
+        scratch_shapes=[
+            pltpu.VMEM(hidden.shape, bf16),
+            pltpu.VMEM((tokens, hidden.shape[2]), bf16),
+            pltpu.VMEM(queries.shape, bf16),
+            pltpu.VMEM(weight.shape, bf16),
+            pltpu.VMEM((4,) + down.shape, bf16),
+            pltpu.VMEM((2, up.shape[2] * 4, up.shape[1]), bf16),
+            pltpu.VMEM((tp, tokens, 2 * down.shape[1]), f32),
+            pltpu.VMEM(cache.shape[1:], bf16),
+            pltpu.VMEM(cache.shape[1:], bf16),
+            pltpu.VMEM((rows * 2 * steps, head_dim), f32),
+            pltpu.VMEM((rows * 2 * steps, head_dim), f32),
+            pltpu.VMEM((kv_here, rows * per_row, head_dim), bf16),
+            pltpu.VMEM((kv_here, rows * per_row, head_dim), f32),
+            pltpu.VMEM((kv_here, rows * per_row, head_dim), f32),
+            pltpu.VMEM((kv_here, rows * per_row, head_dim), f32),
+            dma((3,)),
+            dma((2, W_CHUNKS)),
+            dma((rows,)),
+            dma((rows,)),
+            dma((3, 2)),
+            dma((3, 2)),
+            dma((3,)),
+            dma((3,)),
+            dma((tp - 1,)),
+            dma((tp - 1,)),
+        ],
+        compiler_params=pltpu.CompilerParams(
+            collective_id=0, has_side_effects=True, vmem_limit_bytes=48 * 1024 * 1024
+        ),
+        cost_estimate=pl.CostEstimate(
+            flops=700_000_000, bytes_accessed=moved, transcendentals=800_000
+        ),
+    )(fill, freqs, hidden, queries, weight, down, up, cache)
+
+
+def on_device(*args, mesh):
+    hidden, queries, weight, down, up, cache, _ = args
+    fits = (
+        mesh.shape["fsdp"] == 4
+        and mesh.shape["tp"] > 1
+        and down.shape[2] % 512 == 0
+        and up.shape[2] % 16 == 0
+        and down.shape[1] * 2 == 128
+        and hidden.shape[:2] == (8, 4)
+    )
+    if fits:
+        return on_device_kernel(*args, tp=mesh.shape["tp"])
+    return on_device_plain(*args)
+
 
 def solution(mesh):
     return jax.shard_map(
-        on_device,
+        functools.partial(on_device, mesh=mesh),
         mesh=mesh,
         in_specs=(
             P(("groups", "fsdp"), None, None),

time: 90.9 us -> 27.8 us (0.31)
  the two profiles are of different devices: /device:TPU:0 before, /device:TPU:1 now
where the time goes in v1:
time: 27.8 us; the launch traced here: 27.5 us
  Pallas kernels  20.6 us (74%)
  local copies, waits for them, and re-layouts  6.27 us (23%)
  between operations  0.65 us (2%)
    pallas_call x1, Pallas kernels, on_device_kernel(): pl.pallas_call(kernel, out_shape=(jax.ShapeDtypeStruct((2, rows, steps, w...  20.6 us
    unnamed x13, local copies, waits for them, and re-layouts  6.27 us

profile of v1, /device:TPU:1, one launch (start us, length us, event | category | flops | bytes accessed | tf_op | source)
XLA Modules:
  0.0 27.5 jit_solution(6324937082464352558)
XLA Ops:
  0.6 0.8 %copy.10.up_ref = bf16[2,256,16]{2,1,0:T(8,128)(2,1)S(1)} copy(bf16[2,256,16]{1,2,0:T(8,128)(2,1)} %param.12) | data formatting | bytes 32768 | tf_op args[4]
  1.5 0.0 copy-start
  1.5 1.0 %copy-done = bf16[8,4,8192]{2,1,0:T(4,128)(2,1)S(1)} copy-done((bf16[8,4,8192]{2,1,0:T(4,128)(2,1)S(1)}, bf16[8,4,8192]{2,1,0:T(4,128)(2,1)}, u32[]{:S(2)}) %copy-start) | copy-done | bytes 524312
  2.5 0.0 copy-start.1
  2.5 0.9 %copy-done.1 = bf16[8,4,2048]{2,1,0:T(4,128)(2,1)S(1)} copy-done((bf16[8,4,2048]{2,1,0:T(4,128)(2,1)S(1)}, bf16[8,4,2048]{2,1,0:T(4,128)(2,1)}, u32[]{:S(2)}) %copy-start.1) | copy-done | bytes 131096
  3.4 0.0 copy-start.2
  3.4 0.9 %copy-done.2 = bf16[2,64,512]{2,1,0:T(8,128)(2,1)S(1)} copy-done((bf16[2,64,512]{2,1,0:T(8,128)(2,1)S(1)}, bf16[2,64,512]{2,1,0:T(8,128)(2,1)}, u32[]{:S(2)}) %copy-start.2) | copy-done | bytes 131096
  4.3 0.0 copy-start.3
  4.3 0.7 %copy-done.3 = s32[8]{0:T(128)S(1)} copy-done((s32[8]{0:T(128)S(1)}, s32[8]{0:T(128)}, u32[]{:S(2)}) %copy-start.3) | copy-done | bytes 56
  5.0 0.0 copy-start.4
  5.0 0.7 %copy-done.4 = f32[1,128]{1,0:T(1,128)S(1)} copy-done((f32[1,128]{1,0:T(1,128)S(1)}, f32[1,128]{1,0:T(1,128)}, u32[]{:S(2)}) %copy-start.4) | copy-done | bytes 536
  5.6 20.6 %shard_map.95 = (bf16[2,8,4,256]{3,2,1,0:T(4,128)(2,1)S(1)}, bf16[8,4,2048]{2,1,0:T(4,128)(2,1)S(1)}) custom-call(s32[8]{0:T(128)S(1)} %copy-done.3, f32[1,128]{1,0:T(1,128)S(1)} %copy-done.4, bf16[8,4,8192]{2,1,0:T(4,128)(2,1)S(1)} %copy-done, bf16[8,4,2048]{2,1,0:T(4,128)(2,1)S(1)} %copy-done.1, bf16[2,8192,256]{2,1,0:T(8,128)(2,1)} %weight_hbm.1, ...), custom_call_target="tpu_custom_call" | custom-call | flops 700000000 | bytes 21495808 | tf_op jit(solution)/shard_map/pallas_call | solution.py:400
  26.3 0.6 %copy.13 = bf16[2,8,4,256]{3,2,1,0:T(4,128)(2,1)} copy(bf16[2,8,4,256]{3,2,1,0:T(4,128)(2,1)S(1)} %get-tuple-element.4) | data formatting | bytes 65536
  26.9 0.7 %copy.14 = bf16[8,4,2048]{2,1,0:T(4,128)(2,1)} copy(bf16[8,4,2048]{2,1,0:T(4,128)(2,1)S(1)} %get-tuple-element.5) | data formatting | bytes 262144
Async XLA Ops:
  1.5 1.0 %copy-start = (bf16[8,4,8192]{2,1,0:T(4,128)(2,1)S(1)}, bf16[8,4,8192]{2,1,0:T(4,128)(2,1)}, u32[]{:S(2)}) copy-start(bf16[8,4,8192]{2,1,0:T(4,128)(2,1)} %hidden_hbm.1) | copy-start | bytes 1572868
  2.5 0.9 %copy-start.1 = (bf16[8,4,2048]{2,1,0:T(4,128)(2,1)S(1)}, bf16[8,4,2048]{2,1,0:T(4,128)(2,1)}, u32[]{:S(2)}) copy-start(bf16[8,4,2048]{2,1,0:T(4,128)(2,1)} %queries_hbm.1) | copy-start | bytes 393220
  3.4 0.9 %copy-start.2 = (bf16[2,64,512]{2,1,0:T(8,128)(2,1)S(1)}, bf16[2,64,512]{2,1,0:T(8,128)(2,1)}, u32[]{:S(2)}) copy-start(bf16[2,64,512]{2,1,0:T(8,128)(2,1)} %down_hbm.1) | copy-start | bytes 393220
  4.3 0.7 %copy-start.3 = (s32[8]{0:T(128)S(1)}, s32[8]{0:T(128)}, u32[]{:S(2)}) copy-start(s32[8]{0:T(128)} %fill_ref.1) | copy-start | bytes 100
  5.0 0.7 %copy-start.4 = (f32[1,128]{1,0:T(1,128)S(1)}, f32[1,128]{1,0:T(1,128)}, u32[]{:S(2)}) copy-start(f32[1,128]{1,0:T(1,128)} %constant.2.clone.freq_ref) | copy-start | bytes 1540

commit v2 on v1

--- a/solution.py
+++ b/solution.py
@@ -3,7 +3,6 @@
 
 import jax
 import jax.numpy as jnp
-import numpy as np
 from jax import lax
 from jax.experimental import pallas as pl
 from jax.experimental.pallas import tpu as pltpu
@@ -122,16 +121,16 @@
 
 
 def kernel(
-    fill_ref,
-    freq_ref,
+    fill_hbm,
     hidden_hbm,
     queries_hbm,
     weight_hbm,
     down_hbm,
-    up_ref,
+    up_hbm,
     cache_hbm,
     new_kv_ref,
     attended_ref,
+    fill_ref,
     hidden_raw,
     hidden_flat,
     queries_raw,
@@ -165,7 +164,7 @@
     group = queries_raw.shape[2] // (kv_here * head_dim)
     per_row = group * steps
     part = down.shape[-1]
-    rank_here = up_ref.shape[2]
+    rank_here = up_hbm.shape[1]
     tp = low.shape[0]
     f = lax.axis_index("fsdp")
     t = lax.axis_index("tp")
@@ -174,12 +173,35 @@
     diagonal = sibling + 2 - 4 * (sibling // 2)
     owners = (f, sibling, across, diagonal)
 
+    barrier = pltpu.get_barrier_semaphore()
+    for peer in owners[1:]:
+        pl.semaphore_signal(barrier, inc=1, device_id={"fsdp": peer}, device_id_type=MESH)
+    for d in range(1, tp):
+        pl.semaphore_signal(
+            barrier, inc=1, device_id={"tp": lax.rem(t + d, tp)}, device_id_type=MESH
+        )
+
+    fill_copy = pltpu.make_async_copy(fill_hbm, fill_ref, in_sem.at[3])
+    fill_copy.start()
     hidden_copy = pltpu.make_async_copy(hidden_hbm, hidden_raw, in_sem.at[0])
     hidden_copy.start()
     queries_copy = pltpu.make_async_copy(queries_hbm, queries_raw, in_sem.at[1])
     queries_copy.start()
     down_copy = pltpu.make_async_copy(down_hbm, down.at[0], in_sem.at[2])
     down_copy.start()
+    mine = pl.ds(pl.multiple_of(f * rank_here, rank_here), rank_here)
+    up_copy = pltpu.make_async_copy(up_hbm, up_t.at[:, mine, :], in_sem.at[4])
+    up_copy.start()
+
+    def key_copy(r):
+        return pltpu.make_async_copy(cache_hbm.at[0, r], keys.at[r], key_sem.at[r])
+
+    def value_copy(r):
+        return pltpu.make_async_copy(cache_hbm.at[1, r], values.at[r], value_sem.at[r])
+
+    for r in range(rows // 2):
+        key_copy(r).start()
+        value_copy(r).start()
     depth = width // W_CHUNKS
     weight_copies = []
     for c in range(W_CHUNKS):
@@ -190,19 +212,76 @@
             )
             copy.start()
             weight_copies.append(copy)
-
-    @pl.loop(0, rows)
-    def _(r):
-        pltpu.make_async_copy(cache_hbm.at[0, r], keys.at[r], key_sem.at[r]).start()
-        pltpu.make_async_copy(cache_hbm.at[1, r], values.at[r], value_sem.at[r]).start()
-
-    barrier = pltpu.get_barrier_semaphore()
-    for peer in owners[1:]:
-        pl.semaphore_signal(barrier, inc=1, device_id={"fsdp": peer}, device_id_type=MESH)
-    for d in range(1, tp):
-        pl.semaphore_signal(
-            barrier, inc=1, device_id={"tp": lax.rem(t + d, tp)}, device_id_type=MESH
+    for r in range(rows // 2, rows):
+        key_copy(r).start()
+        value_copy(r).start()
+
+    lane = lax.broadcasted_iota(jnp.int32, (1, head_dim), 1)
+    sign = jnp.where(lane < half, -1.0, 1.0).astype(jnp.float32)
+    freq = jnp.ones((1, head_dim), jnp.float32)
+    for bit in range(half.bit_length() - 1):
+        step = rope_theta ** (-2.0 * 2**bit / head_dim)
+        freq = jnp.where((lane >> bit) & 1 == 1, freq * step, freq)
+
+    fill_copy.wait()
+
+    def tables(count, each):
+        at = lax.broadcasted_iota(jnp.int32, (count, head_dim), 0)
+        position = lax.rem(at, steps)
+        for r in range(rows):
+            position = position + jnp.where(at // each == r, fill_ref[r], 0)
+        angle = position.astype(jnp.float32) * freq
+        return jnp.cos(angle), jnp.sin(angle) * sign
+
+    cos_all, sin_all = tables(rows * 2 * steps, 2 * steps)
+    cos_q[...] = cos_all
+    sin_q[...] = sin_all
+    cos_k, sin_k = tables(tokens, steps)
+
+    hidden_copy.wait()
+    block = 512
+    for c in range(width // block):
+        span = slice(c * block, (c + 1) * block)
+        hidden_flat[:, span] = (
+            hidden_raw[:, :, span].astype(jnp.float32).reshape(tokens, block).astype(jnp.bfloat16)
         )
+
+    factor = math.log2(math.e) / math.sqrt(head_dim)
+    slot_at = lax.broadcasted_iota(jnp.int32, (1, slots), 1)
+
+    def attend(pair):
+        chains = []
+        for r in pair:
+            table = slice(r * 2 * steps, (r + 1) * 2 * steps)
+            cosine = jnp.concatenate([cos_q[table, :]] * (group // 2), axis=0)
+            sine = jnp.concatenate([sin_q[table, :]] * (group // 2), axis=0)
+            row = queries_raw[r].astype(jnp.float32)
+            bias = jnp.where(slot_at < fill_ref[r], 0.0, -1e30)
+            for k in range(kv_here):
+                heads = range(k * group, (k + 1) * group)
+                q = jnp.concatenate(
+                    [row[:, h * head_dim : (h + 1) * head_dim] for h in heads], axis=0
+                )
+                q = (q * cosine + pltpu.roll(q, half, 1) * sine).astype(jnp.bfloat16)
+                here = slice(r * per_row, (r + 1) * per_row)
+                q_rot[k, here, :] = q
+                chains.append((r, k, here, q, bias))
+        for r in pair:
+            key_copy(r).wait()
+            value_copy(r).wait()
+        scores = [dot_nt(q, keys[r, k]) + bias for r, k, here, q, bias in chains]
+        for (r, k, here, q, bias), score in zip(chains, scores):
+            peak = jnp.max(score, axis=1, keepdims=True)
+            expo = jnp.exp2((score - peak) * factor)
+            out_acc[k, here, :] = dot_nn(expo.astype(jnp.bfloat16), values[r, k])
+            peak_acc[k, here, :] = jnp.broadcast_to(peak, (per_row, head_dim))
+            total = jnp.sum(expo, axis=1, keepdims=True)
+            sum_acc[k, here, :] = jnp.broadcast_to(total, (per_row, head_dim))
+
+    quarter = rows // 4
+    queries_copy.wait()
+    attend(range(quarter))
+
     pl.semaphore_wait(barrier, 3 + tp - 1)
 
     def send_down(source, slot, z, peer, sem):
@@ -221,17 +300,10 @@
     for copy in to_across + to_sibling:
         copy.start()
 
-    mine = pl.ds(pl.multiple_of(f * rank_here, rank_here), rank_here)
-    eye = (
-        lax.broadcasted_iota(jnp.int32, (rank_here, rank_here), 0)
-        == lax.broadcasted_iota(jnp.int32, (rank_here, rank_here), 1)
-    ).astype(jnp.float32).astype(jnp.bfloat16)
-    for z in range(2):
-        up_t[z, mine, :] = dot_nt(eye, up_ref[z]).astype(jnp.bfloat16)
     up_copies = []
     for n, peer in enumerate(owners[1:]):
         copy = pltpu.make_async_remote_copy(
-            src_ref=up_t.at[:, mine, :],
+            src_ref=up_hbm,
             dst_ref=up_t.at[:, mine, :],
             send_sem=up_send.at[n],
             recv_sem=up_recv.at[n],
@@ -240,31 +312,7 @@
         )
         copy.start()
         up_copies.append(copy)
-
-    lane = lax.broadcasted_iota(jnp.int32, (1, head_dim), 1)
-    sign = jnp.where(lane < half, -1.0, 1.0).astype(jnp.float32)
-    freq = freq_ref[...]
-
-    def tables(count, each):
-        at = lax.broadcasted_iota(jnp.int32, (count, head_dim), 0)
-        position = lax.rem(at, steps)
-        for r in range(rows):
-            position = position + jnp.where(at // each == r, fill_ref[r], 0)
-        angle = position.astype(jnp.float32) * freq
-        return jnp.cos(angle), jnp.sin(angle) * sign
-
-    cos_all, sin_all = tables(rows * 2 * steps, 2 * steps)
-    cos_q[...] = cos_all
-    sin_q[...] = sin_all
-    cos_k, sin_k = tables(tokens, steps)
-
-    hidden_copy.wait()
-    block = 512
-    for c in range(width // block):
-        span = slice(c * block, (c + 1) * block)
-        hidden_flat[:, span] = (
-            hidden_raw[:, :, span].astype(jnp.float32).reshape(tokens, block).astype(jnp.bfloat16)
-        )
+    attend(range(quarter, 2 * quarter))
 
     base = [jnp.zeros((tokens, weight.shape[2]), jnp.float32) for _ in range(2)]
     for c in range(W_CHUNKS):
@@ -273,23 +321,20 @@
             span = slice(c * depth, (c + 1) * depth)
             base[z] = base[z] + dot_nn(hidden_flat[:, span], weight[z, span, :])
 
+    for z in range(2):
+        to_across[z].wait_recv()
+        forward[z].start()
+    attend(range(2 * quarter, 3 * quarter))
+
     def low_of(slot):
         span = pl.ds(pl.multiple_of((owners[slot] * tp + t) * part, part), part)
         factors = down[slot].reshape(down.shape[1] * down.shape[2], part)
         return dot_nt(hidden_flat[:, span], factors)
 
     down_copy.wait()
-    partial = low_of(0)
-    for z in range(2):
-        to_sibling[z].wait_recv()
-    partial = partial + low_of(1)
-    for z in range(2):
-        to_across[z].wait_recv()
-        forward[z].start()
-    partial = partial + low_of(2)
-    for z in range(2):
-        forward[z].wait_recv()
-    partial = partial + low_of(3)
+    for copy in to_sibling + forward:
+        copy.wait_recv()
+    partial = (low_of(0) + low_of(1)) + (low_of(2) + low_of(3))
     low[t] = partial
     low_copies = []
     for d in range(1, tp):
@@ -304,40 +349,13 @@
         copy.start()
         low_copies.append(copy)
 
-    queries_copy.wait()
-    factor = math.log2(math.e) / math.sqrt(head_dim)
-    slot_at = lax.broadcasted_iota(jnp.int32, (per_row, slots), 1)
-
-    @pl.loop(0, rows)
-    def _(r):
-        table = pl.ds(pl.multiple_of(r * 2 * steps, 2 * steps), 2 * steps)
-        cosine = jnp.concatenate([cos_q[table, :]] * (group // 2), axis=0)
-        sine = jnp.concatenate([sin_q[table, :]] * (group // 2), axis=0)
-        here = pl.ds(pl.multiple_of(r * per_row, per_row), per_row)
-        row = queries_raw[r].astype(jnp.float32)
-        live = slot_at < fill_ref[r]
-        pltpu.make_async_copy(cache_hbm.at[0, r], keys.at[r], key_sem.at[r]).wait()
-        pltpu.make_async_copy(cache_hbm.at[1, r], values.at[r], value_sem.at[r]).wait()
-        for k in range(kv_here):
-            first = k * group
-            q = jnp.concatenate(
-                [row[:, (first + g) * head_dim : (first + g + 1) * head_dim] for g in range(group)],
-                axis=0,
-            )
-            q = (q * cosine + pltpu.roll(q, half, 1) * sine).astype(jnp.bfloat16)
-            q_rot[k, here, :] = q
-            scores = jnp.where(live, dot_nt(q, keys[r, k]), -1e30)
-            peak = jnp.max(scores, axis=1, keepdims=True)
-            expo = jnp.exp2((scores - peak) * factor)
-            out_acc[k, here, :] = dot_nn(expo.astype(jnp.bfloat16), values[r, k])
-            peak_acc[k, here, :] = jnp.broadcast_to(peak, (per_row, head_dim))
-            total = jnp.sum(expo, axis=1, keepdims=True)
-            sum_acc[k, here, :] = jnp.broadcast_to(total, (per_row, head_dim))
+    attend(range(3 * quarter, rows))
 
     for copy in low_copies:
         copy.wait_recv()
     for copy in up_copies:
         copy.wait_recv()
+    up_copy.wait()
     low_all = low[0]
     for d in range(1, tp):
         low_all = low_all + low[d]
@@ -390,9 +408,7 @@
     tokens = rows * steps
     kv_here, head_dim = cache.shape[2], cache.shape[4]
     per_row = queries.shape[2] // (kv_here * head_dim) * steps
-    freqs = rope_theta ** (-2.0 * (np.arange(head_dim) % (head_dim // 2)) / head_dim)
-    freqs = jnp.asarray(freqs[None, :], jnp.float32)
-    any_spec = pl.BlockSpec(memory_space=pl.ANY)
+    hbm_spec = pl.BlockSpec(memory_space=pltpu.HBM)
     vmem_spec = pl.BlockSpec(memory_space=pltpu.VMEM)
     dma = pltpu.SemaphoreType.DMA
     f32, bf16 = jnp.float32, jnp.bfloat16
@@ -403,18 +419,10 @@
             jax.ShapeDtypeStruct((2, rows, steps, weight.shape[2]), bf16),
             jax.ShapeDtypeStruct(queries.shape, bf16),
         ),
-        in_specs=[
-            pl.BlockSpec(memory_space=pltpu.SMEM),
-            vmem_spec,
-            any_spec,
-            any_spec,
-            any_spec,
-            any_spec,
-            vmem_spec,
-            any_spec,
-        ],
+        in_specs=[hbm_spec] * 7,
         out_specs=(vmem_spec, vmem_spec),
         scratch_shapes=[
+            pltpu.SMEM(fill.shape, jnp.int32),
             pltpu.VMEM(hidden.shape, bf16),
             pltpu.VMEM((tokens, hidden.shape[2]), bf16),
             pltpu.VMEM(queries.shape, bf16),
@@ -430,7 +438,7 @@
             pltpu.VMEM((kv_here, rows * per_row, head_dim), f32),
             pltpu.VMEM((kv_here, rows * per_row, head_dim), f32),
             pltpu.VMEM((kv_here, rows * per_row, head_dim), f32),
-            dma((3,)),
+            dma((5,)),
             dma((2, W_CHUNKS)),
             dma((rows,)),
             dma((rows,)),
@@ -442,12 +450,12 @@
             dma((tp - 1,)),
         ],
         compiler_params=pltpu.CompilerParams(
-            collective_id=0, has_side_effects=True, vmem_limit_bytes=48 * 1024 * 1024
+            collective_id=0, has_side_effects=True, vmem_limit_bytes=64 * 1024 * 1024
         ),
         cost_estimate=pl.CostEstimate(
             flops=700_000_000, bytes_accessed=moved, transcendentals=800_000
         ),
-    )(fill, freqs, hidden, queries, weight, down, up, cache)
+    )(fill, hidden, queries, weight, down, jnp.swapaxes(up, 1, 2), cache)
 
 
 def on_device(*args, mesh):

time: 27.8 us -> 25.4 us (0.914)
  the two profiles are of different devices: /device:TPU:1 before, /device:TPU:0 now
where the time goes in v2:
time: 25.4 us; the launch traced here: 25.2 us
  Pallas kernels  21.6 us (85%)
  local copies, waits for them, and re-layouts  2.99 us (12%)
  between operations  0.64 us (3%)
    pallas_call x1, Pallas kernels, on_device_kernel(): pl.pallas_call(kernel, out_shape=(jax.ShapeDtypeStruct((2, rows, steps, w...  21.6 us
    unnamed x2, local copies, waits for them, and re-layouts  2.99 us

profile of v2, /device:TPU:0, one launch (start us, length us, event | category | flops | bytes accessed | tf_op | source)
XLA Modules:
  0.0 25.2 jit_solution(319705346681035205)
XLA Ops:
  0.6 21.6 %shard_map.86 = (bf16[2,8,4,256]{3,2,1,0:T(4,128)(2,1)}, bf16[8,4,2048]{2,1,0:T(4,128)(2,1)}) custom-call(s32[8]{0:T(128)} %fill_hbm.1, bf16[8,4,8192]{2,1,0:T(4,128)(2,1)} %hidden_hbm.1, bf16[8,4,2048]{2,1,0:T(4,128)(2,1)} %queries_hbm.1, bf16[2,8192,256]{2,1,0:T(8,128)(2,1)} %weight_hbm.1, bf16[2,64,512]{2,1,0:T(8,128)(2,1)} %down_hbm.1, ...), custom_call_target="tpu_custom_call" | custom-call | flops 700000000 | bytes 21495808 | tf_op jit(solution)/shard_map/pallas_call | solution.py:416
  22.2 1.4 %copy.11 = bf16[2,8,4,256]{3,2,1,0:T(4,128)(2,1)} copy(bf16[2,8,4,256]{3,2,1,0:T(4,128)(2,1)} %get-tuple-element.4) | data formatting | bytes 65536
  23.6 1.6 %copy.12 = bf16[8,4,2048]{2,1,0:T(4,128)(2,1)} copy(bf16[8,4,2048]{2,1,0:T(4,128)(2,1)} %get-tuple-element.5) | data formatting | bytes 262144

commit v3 on v2

--- a/solution.py
+++ b/solution.py
@@ -109,6 +109,7 @@
 
 MESH = pl.DeviceIdType.MESH
 W_CHUNKS = 4
+CACHE_CHUNKS = 4
 NT = (((1,), (1,)), ((), ()))
 
 
@@ -118,51 +119,54 @@
 
 def dot_nn(a, b):
     return jnp.dot(a, b, preferred_element_type=jnp.float32)
+
+
+def rotation_tables(fill_ref, rows, each, steps, head_dim):
+    half = head_dim // 2
+    lane = lax.broadcasted_iota(jnp.int32, (1, head_dim), 1)
+    sign = jnp.where(lane < half, -1.0, 1.0).astype(jnp.float32)
+    freq = jnp.ones((1, head_dim), jnp.float32)
+    for bit in range(half.bit_length() - 1):
+        step = rope_theta ** (-2.0 * 2**bit / head_dim)
+        freq = jnp.where((lane >> bit) & 1 == 1, freq * step, freq)
+    at = lax.broadcasted_iota(jnp.int32, (rows * each, head_dim), 0)
+    position = lax.rem(at, steps)
+    for r in range(rows):
+        position = position + jnp.where(at // each == r, fill_ref[r], 0)
+    angle = position.astype(jnp.float32) * freq
+    return jnp.cos(angle), jnp.sin(angle) * sign
 
 
 def kernel(
     fill_hbm,
     hidden_hbm,
-    queries_hbm,
     weight_hbm,
     down_hbm,
     up_hbm,
-    cache_hbm,
-    new_kv_ref,
-    attended_ref,
+    new_hbm,
     fill_ref,
     hidden_raw,
     hidden_flat,
-    queries_raw,
     weight,
     down,
     up_t,
     low,
-    keys,
-    values,
-    cos_q,
-    sin_q,
-    q_rot,
-    out_acc,
-    peak_acc,
-    sum_acc,
+    new_acc,
     in_sem,
     weight_sem,
-    key_sem,
-    value_sem,
     down_send,
     down_recv,
     up_send,
     up_recv,
     low_send,
     low_recv,
+    *,
+    head_dim,
 ):
     rows, steps, width = hidden_raw.shape
     tokens = rows * steps
-    kv_here, slots, head_dim = keys.shape[1], keys.shape[2], keys.shape[3]
+    kv_here = weight.shape[2] // head_dim
     half = head_dim // 2
-    group = queries_raw.shape[2] // (kv_here * head_dim)
-    per_row = group * steps
     part = down.shape[-1]
     rank_here = up_hbm.shape[1]
     tp = low.shape[0]
@@ -185,23 +189,12 @@
     fill_copy.start()
     hidden_copy = pltpu.make_async_copy(hidden_hbm, hidden_raw, in_sem.at[0])
     hidden_copy.start()
-    queries_copy = pltpu.make_async_copy(queries_hbm, queries_raw, in_sem.at[1])
-    queries_copy.start()
     down_copy = pltpu.make_async_copy(down_hbm, down.at[0], in_sem.at[2])
     down_copy.start()
     mine = pl.ds(pl.multiple_of(f * rank_here, rank_here), rank_here)
     up_copy = pltpu.make_async_copy(up_hbm, up_t.at[:, mine, :], in_sem.at[4])
     up_copy.start()
 
-    def key_copy(r):
-        return pltpu.make_async_copy(cache_hbm.at[0, r], keys.at[r], key_sem.at[r])
-
-    def value_copy(r):
-        return pltpu.make_async_copy(cache_hbm.at[1, r], values.at[r], value_sem.at[r])
-
-    for r in range(rows // 2):
-        key_copy(r).start()
-        value_copy(r).start()
     depth = width // W_CHUNKS
     weight_copies = []
     for c in range(W_CHUNKS):
@@ -212,76 +205,6 @@
             )
             copy.start()
             weight_copies.append(copy)
-    for r in range(rows // 2, rows):
-        key_copy(r).start()
-        value_copy(r).start()
-
-    lane = lax.broadcasted_iota(jnp.int32, (1, head_dim), 1)
-    sign = jnp.where(lane < half, -1.0, 1.0).astype(jnp.float32)
-    freq = jnp.ones((1, head_dim), jnp.float32)
-    for bit in range(half.bit_length() - 1):
-        step = rope_theta ** (-2.0 * 2**bit / head_dim)
-        freq = jnp.where((lane >> bit) & 1 == 1, freq * step, freq)
-
-    fill_copy.wait()
-
-    def tables(count, each):
-        at = lax.broadcasted_iota(jnp.int32, (count, head_dim), 0)
-        position = lax.rem(at, steps)
-        for r in range(rows):
-            position = position + jnp.where(at // each == r, fill_ref[r], 0)
-        angle = position.astype(jnp.float32) * freq
-        return jnp.cos(angle), jnp.sin(angle) * sign
-
-    cos_all, sin_all = tables(rows * 2 * steps, 2 * steps)
-    cos_q[...] = cos_all
-    sin_q[...] = sin_all
-    cos_k, sin_k = tables(tokens, steps)
-
-    hidden_copy.wait()
-    block = 512
-    for c in range(width // block):
-        span = slice(c * block, (c + 1) * block)
-        hidden_flat[:, span] = (
-            hidden_raw[:, :, span].astype(jnp.float32).reshape(tokens, block).astype(jnp.bfloat16)
-        )
-
-    factor = math.log2(math.e) / math.sqrt(head_dim)
-    slot_at = lax.broadcasted_iota(jnp.int32, (1, slots), 1)
-
-    def attend(pair):
-        chains = []
-        for r in pair:
-            table = slice(r * 2 * steps, (r + 1) * 2 * steps)
-            cosine = jnp.concatenate([cos_q[table, :]] * (group // 2), axis=0)
-            sine = jnp.concatenate([sin_q[table, :]] * (group // 2), axis=0)
-            row = queries_raw[r].astype(jnp.float32)
-            bias = jnp.where(slot_at < fill_ref[r], 0.0, -1e30)
-            for k in range(kv_here):
-                heads = range(k * group, (k + 1) * group)
-                q = jnp.concatenate(
-                    [row[:, h * head_dim : (h + 1) * head_dim] for h in heads], axis=0
-                )
-                q = (q * cosine + pltpu.roll(q, half, 1) * sine).astype(jnp.bfloat16)
-                here = slice(r * per_row, (r + 1) * per_row)
-                q_rot[k, here, :] = q
-                chains.append((r, k, here, q, bias))
-        for r in pair:
-            key_copy(r).wait()
-            value_copy(r).wait()
-        scores = [dot_nt(q, keys[r, k]) + bias for r, k, here, q, bias in chains]
-        for (r, k, here, q, bias), score in zip(chains, scores):
-            peak = jnp.max(score, axis=1, keepdims=True)
-            expo = jnp.exp2((score - peak) * factor)
-            out_acc[k, here, :] = dot_nn(expo.astype(jnp.bfloat16), values[r, k])
-            peak_acc[k, here, :] = jnp.broadcast_to(peak, (per_row, head_dim))
-            total = jnp.sum(expo, axis=1, keepdims=True)
-            sum_acc[k, here, :] = jnp.broadcast_to(total, (per_row, head_dim))
-
-    quarter = rows // 4
-    queries_copy.wait()
-    attend(range(quarter))
-
     pl.semaphore_wait(barrier, 3 + tp - 1)
 
     def send_down(source, slot, z, peer, sem):
@@ -312,8 +235,15 @@
         )
         copy.start()
         up_copies.append(copy)
-    attend(range(quarter, 2 * quarter))
-
+    fill_copy.wait()
+    cos_k, sin_k = rotation_tables(fill_ref, rows, steps, steps, head_dim)
+    hidden_copy.wait()
+    block = 512
+    for c in range(width // block):
+        span = slice(c * block, (c + 1) * block)
+        hidden_flat[:, span] = (
+            hidden_raw[:, :, span].astype(jnp.float32).reshape(tokens, block).astype(jnp.bfloat16)
+        )
     base = [jnp.zeros((tokens, weight.shape[2]), jnp.float32) for _ in range(2)]
     for c in range(W_CHUNKS):
         for z in range(2):
@@ -324,8 +254,6 @@
     for z in range(2):
         to_across[z].wait_recv()
         forward[z].start()
-    attend(range(2 * quarter, 3 * quarter))
-
     def low_of(slot):
         span = pl.ds(pl.multiple_of((owners[slot] * tp + t) * part, part), part)
         factors = down[slot].reshape(down.shape[1] * down.shape[2], part)
@@ -349,8 +277,6 @@
         copy.start()
         low_copies.append(copy)
 
-    attend(range(3 * quarter, rows))
-
     for copy in low_copies:
         copy.wait_recv()
     for copy in up_copies:
@@ -368,7 +294,114 @@
         factors = up_t[z]
         update = dot_nn(high, factors) + dot_nn(rest, factors)
         proj.append(base[z] + adapter_scale * update)
-    count = rows * per_row
+    for k in range(kv_here):
+        columns = slice(k * head_dim, (k + 1) * head_dim)
+        key = proj[0][:, columns]
+        new_acc[0, :, columns] = key * cos_k + pltpu.roll(key, half, 1) * sin_k
+    new_acc[1] = proj[1]
+    new_copy = pltpu.make_async_copy(new_acc, new_hbm, in_sem.at[5])
+    new_copy.start()
+    new_copy.wait()
+    for copy in to_across + to_sibling + forward + up_copies + low_copies:
+        copy.wait_send()
+
+
+def attention_kernel(
+    fill_ref,
+    new_hbm,
+    queries_hbm,
+    cache_hbm,
+    new_kv_ref,
+    attended_ref,
+    new_raw,
+    queries_raw,
+    keys,
+    values,
+    cos_q,
+    sin_q,
+    q_rot,
+    out_acc,
+    peak_acc,
+    sum_acc,
+    in_sem,
+    key_sem,
+    value_sem,
+):
+    rows, steps = attended_ref.shape[:2]
+    tokens = rows * steps
+    kv_here, slots, head_dim = keys.shape[1:]
+    count = q_rot.shape[1]
+    per_row = count // rows
+    group = per_row // steps
+    half = head_dim // 2
+    chunk = slots // CACHE_CHUNKS
+    factor = math.log2(math.e) / math.sqrt(head_dim)
+
+    queries_copy = pltpu.make_async_copy(queries_hbm, queries_raw, in_sem.at[0])
+    queries_copy.start()
+
+    def chunk_copies(r, c):
+        span = pl.ds(c * chunk, chunk)
+        return (
+            pltpu.make_async_copy(
+                cache_hbm.at[0, r, :, span], keys.at[r, :, span], key_sem.at[r, c]
+            ),
+            pltpu.make_async_copy(
+                cache_hbm.at[1, r, :, span], values.at[r, :, span], value_sem.at[r, c]
+            ),
+        )
+
+    for r in range(rows):
+        for c in range(CACHE_CHUNKS):
+
+            @pl.when(c * chunk < fill_ref[r])
+            def _():
+                for copy in chunk_copies(r, c):
+                    copy.start()
+
+    new_copy = pltpu.make_async_copy(new_hbm, new_raw, in_sem.at[1])
+    new_copy.start()
+    cos_all, sin_all = rotation_tables(fill_ref, rows, 2 * steps, steps, head_dim)
+    cos_q[...] = cos_all
+    sin_q[...] = sin_all
+    queries_copy.wait()
+    for r in range(rows):
+        table = slice(r * 2 * steps, (r + 1) * 2 * steps)
+        cosine = jnp.concatenate([cos_q[table, :]] * (group // 2), axis=0)
+        sine = jnp.concatenate([sin_q[table, :]] * (group // 2), axis=0)
+        row = queries_raw[r].astype(jnp.float32)
+        for k in range(kv_here):
+            heads = range(k * group, (k + 1) * group)
+            q = jnp.concatenate([row[:, h * head_dim : (h + 1) * head_dim] for h in heads], axis=0)
+            q = q * cosine + pltpu.roll(q, half, 1) * sine
+            q_rot[k, r * per_row : (r + 1) * per_row, :] = q.astype(jnp.bfloat16)
+
+    @pl.loop(0, rows)
+    def _(r):
+        filled = fill_ref[r]
+        here = pl.ds(pl.multiple_of(r * per_row, per_row), per_row)
+        for used in range(1, CACHE_CHUNKS + 1):
+
+            @pl.when(((used - 1) * chunk < filled) & (filled <= used * chunk))
+            def _():
+                for c in range(used):
+                    for copy in chunk_copies(r, c):
+                        copy.wait()
+                length = used * chunk
+                slot_at = lax.broadcasted_iota(jnp.int32, (1, length), 1)
+                bias = jnp.where(slot_at < filled, 0.0, -1e30)
+                scores = [
+                    dot_nt(q_rot[k, here, :], keys[r, k, :length]) + bias for k in range(kv_here)
+                ]
+                for k, score in enumerate(scores):
+                    peak = jnp.max(score, axis=1, keepdims=True)
+                    expo = jnp.exp2((score - peak) * factor)
+                    out_acc[k, here, :] = dot_nn(expo.astype(jnp.bfloat16), values[r, k, :length])
+                    peak_acc[k, here, :] = jnp.broadcast_to(peak, (per_row, head_dim))
+                    total = jnp.sum(expo, axis=1, keepdims=True)
+                    sum_acc[k, here, :] = jnp.broadcast_to(total, (per_row, head_dim))
+
+    new_copy.wait()
     row_at = lax.broadcasted_iota(jnp.int32, (count, tokens), 0)
     col_at = lax.broadcasted_iota(jnp.int32, (count, tokens), 1)
     seen = (row_at // per_row == col_at // steps) & (
@@ -376,9 +409,8 @@
     )
     for k in range(kv_here):
         columns = slice(k * head_dim, (k + 1) * head_dim)
-        key = proj[0][:, columns]
-        key = key * cos_k + pltpu.roll(key, half, 1) * sin_k
-        value = proj[1][:, columns]
+        key = new_raw[0, :, columns]
+        value = new_raw[1, :, columns]
         for r in range(rows):
             span = slice(r * steps, (r + 1) * steps)
             new_kv_ref[0, r, :, columns] = key[span].astype(jnp.bfloat16)
@@ -399,9 +431,6 @@
                     at : at + steps
                 ].astype(jnp.bfloat16)
 
-    for copy in to_across + to_sibling + forward + up_copies + low_copies:
-        copy.wait_send()
-
 
 def on_device_kernel(hidden, queries, weight, down, up, cache, fill, tp):
     rows, steps, _ = hidden.shape
@@ -412,36 +441,24 @@
     vmem_spec = pl.BlockSpec(memory_space=pltpu.VMEM)
     dma = pltpu.SemaphoreType.DMA
     f32, bf16 = jnp.float32, jnp.bfloat16
-    moved = sum(math.prod(a.shape) * 2 for a in (hidden, weight, cache))
-    return pl.pallas_call(
-        kernel,
-        out_shape=(
-            jax.ShapeDtypeStruct((2, rows, steps, weight.shape[2]), bf16),
-            jax.ShapeDtypeStruct(queries.shape, bf16),
-        ),
-        in_specs=[hbm_spec] * 7,
-        out_specs=(vmem_spec, vmem_spec),
+    moved = sum(math.prod(a.shape) * 2 for a in (hidden, weight))
+    held = (kv_here, rows * per_row, head_dim)
+    projected = pl.pallas_call(
+        functools.partial(kernel, head_dim=head_dim),
+        out_shape=jax.ShapeDtypeStruct((2, tokens, weight.shape[2]), f32),
+        in_specs=[hbm_spec] * 5,
+        out_specs=hbm_spec,
         scratch_shapes=[
             pltpu.SMEM(fill.shape, jnp.int32),
             pltpu.VMEM(hidden.shape, bf16),
             pltpu.VMEM((tokens, hidden.shape[2]), bf16),
-            pltpu.VMEM(queries.shape, bf16),
             pltpu.VMEM(weight.shape, bf16),
             pltpu.VMEM((4,) + down.shape, bf16),
             pltpu.VMEM((2, up.shape[2] * 4, up.shape[1]), bf16),
             pltpu.VMEM((tp, tokens, 2 * down.shape[1]), f32),
-            pltpu.VMEM(cache.shape[1:], bf16),
-            pltpu.VMEM(cache.shape[1:], bf16),
-            pltpu.VMEM((rows * 2 * steps, head_dim), f32),
-            pltpu.VMEM((rows * 2 * steps, head_dim), f32),
-            pltpu.VMEM((kv_here, rows * per_row, head_dim), bf16),
-            pltpu.VMEM((kv_here, rows * per_row, head_dim), f32),
-            pltpu.VMEM((kv_here, rows * per_row, head_dim), f32),
-            pltpu.VMEM((kv_here, rows * per_row, head_dim), f32),
-            dma((5,)),
+            pltpu.VMEM((2, tokens, weight.shape[2]), f32),
+            dma((6,)),
             dma((2, W_CHUNKS)),
-            dma((rows,)),
-            dma((rows,)),
             dma((3, 2)),
             dma((3, 2)),
             dma((3,)),
@@ -455,7 +472,32 @@
         cost_estimate=pl.CostEstimate(
             flops=700_000_000, bytes_accessed=moved, transcendentals=800_000
         ),
-    )(fill, hidden, queries, weight, down, jnp.swapaxes(up, 1, 2), cache)
+    )(fill, hidden, weight, down, jnp.swapaxes(up, 1, 2))
+    return pl.pallas_call(
+        attention_kernel,
+        out_shape=(
+            jax.ShapeDtypeStruct((2, rows, steps, weight.shape[2]), bf16),
+            jax.ShapeDtypeStruct(queries.shape, bf16),
+        ),
+        in_specs=[pl.BlockSpec(memory_space=pltpu.SMEM)] + [hbm_spec] * 3,
+        out_specs=(vmem_spec, vmem_spec),
+        scratch_shapes=[
+            pltpu.VMEM((2, tokens, weight.shape[2]), f32),
+            pltpu.VMEM(queries.shape, bf16),
+            pltpu.VMEM(cache.shape[1:], bf16),
+            pltpu.VMEM(cache.shape[1:], bf16),
+            pltpu.VMEM((rows * 2 * steps, head_dim), f32),
+            pltpu.VMEM((rows * 2 * steps, head_dim), f32),
+            pltpu.VMEM(held, bf16),
+            pltpu.VMEM(held, f32),
+            pltpu.VMEM(held, f32),
+            pltpu.VMEM(held, f32),
+            dma((2,)),
+            dma((rows, CACHE_CHUNKS)),
+            dma((rows, CACHE_CHUNKS)),
+        ],
+        compiler_params=pltpu.CompilerParams(vmem_limit_bytes=64 * 1024 * 1024),
+    )(fill, projected, queries, cache)
 
 
 def on_device(*args, mesh):
@@ -466,6 +508,7 @@
         and down.shape[2] % 512 == 0
         and up.shape[2] % 16 == 0
         and down.shape[1] * 2 == 128
+        and cache.shape[3] % (16 * CACHE_CHUNKS) == 0
         and hidden.shape[:2] == (8, 4)
     )
     if fits:

time: 25.4 us -> 26.4 us (1.039); the launches traced: 25.2 us -> 26.9 us
  Pallas kernels: 21.6 us -> 26.3 us
  local copies, waits for them, and re-layouts: 2.99 us -> 0 us
    pallas_call x1 -> x2, Pallas kernels: 21.6 us -> 26.3 us  [the longest x1 14.8 us: on_device_kernel(): pl.pallas_call(functools.partial(kernel, head_dim=head_dim), out_shape=ja...]
    unnamed x2 -> x0, local copies, waits for them, and re-layouts: 2.99 us -> none
where the time goes in v3:
time: 26.4 us; the launch traced here: 26.9 us
  Pallas kernels  26.3 us (100%)
  between operations  0.64 us (2%)
    pallas_call x1, Pallas kernels, on_device_kernel(): pl.pallas_call(functools.partial(kernel, head_dim=head_dim), out_shape=ja...  14.8 us
    pallas_call x1, Pallas kernels, on_device_kernel(): pl.pallas_call(attention_kernel, out_shape=(jax.ShapeDtypeStruct((2, rows...  11.4 us

profile of v3, /device:TPU:0, one launch (start us, length us, event | category | flops | bytes accessed | tf_op | source)
XLA Modules:
  0.0 26.9 jit_solution(5870729005903154348)
XLA Ops:
  0.6 14.8 %shard_map.86.new_hbm = f32[2,32,256]{2,1,0:T(8,128)} custom-call(s32[8]{0:T(128)} %fill_ref.1, bf16[8,4,8192]{2,1,0:T(4,128)(2,1)} %hidden_hbm.1, bf16[2,8192,256]{2,1,0:T(8,128)(2,1)} %weight_hbm.1, bf16[2,64,512]{2,1,0:T(8,128)(2,1)} %down_hbm.1, bf16[2,16,256]{2,1,0:T(8,128)(2,1)} %bitcast.1), custom_call_target="tpu_custom_call" | custom-call | flops 700000000 | bytes 8912896 | tf_op jit(solution)/shard_map/pallas_call | solution.py:446
  15.5 11.4 %shard_map.87 = (bf16[2,8,4,256]{3,2,1,0:T(4,128)(2,1)}, bf16[8,4,2048]{2,1,0:T(4,128)(2,1)}) custom-call(s32[8]{0:T(128)} %fill_ref.1, f32[2,32,256]{2,1,0:T(8,128)} %shard_map.86.new_hbm, bf16[8,4,2048]{2,1,0:T(4,128)(2,1)} %queries_hbm.1, bf16[2,8,2,1536,128]{4,3,2,1,0:T(8,128)(2,1)} %cache_hbm.1), custom_call_target="tpu_custom_call" | custom-call | tf_op jit(solution)/shard_map/pallas_call | solution.py:476

commit v4 on v2

--- a/solution.py
+++ b/solution.py
@@ -128,8 +128,11 @@
     down_hbm,
     up_hbm,
     cache_hbm,
-    new_kv_ref,
-    attended_ref,
+    new_hbm,
+    q_hbm,
+    out_hbm,
+    peak_hbm,
+    sum_hbm,
     fill_ref,
     hidden_raw,
     hidden_flat,
@@ -146,6 +149,7 @@
     out_acc,
     peak_acc,
     sum_acc,
+    new_acc,
     in_sem,
     weight_sem,
     key_sem,
@@ -156,6 +160,7 @@
     up_recv,
     low_send,
     low_recv,
+    out_sem,
 ):
     rows, steps, width = hidden_raw.shape
     tokens = rows * steps
@@ -248,6 +253,8 @@
 
     factor = math.log2(math.e) / math.sqrt(head_dim)
     slot_at = lax.broadcasted_iota(jnp.int32, (1, slots), 1)
+
+    out_copies = []
 
     def attend(pair):
         chains = []
@@ -277,10 +284,17 @@
             peak_acc[k, here, :] = jnp.broadcast_to(peak, (per_row, head_dim))
             total = jnp.sum(expo, axis=1, keepdims=True)
             sum_acc[k, here, :] = jnp.broadcast_to(total, (per_row, head_dim))
+        span = slice(pair[0] * per_row, (pair[-1] + 1) * per_row)
+        held = ((q_rot, q_hbm), (out_acc, out_hbm), (peak_acc, peak_hbm), (sum_acc, sum_hbm))
+        for n, (source, target) in enumerate(held):
+            copy = pltpu.make_async_copy(
+                source.at[:, span, :], target.at[:, span, :], out_sem.at[pair[0], n]
+            )
+            copy.start()
+            out_copies.append(copy)
 
     quarter = rows // 4
     queries_copy.wait()
-    attend(range(quarter))
 
     pl.semaphore_wait(barrier, 3 + tp - 1)
 
@@ -312,6 +326,7 @@
         )
         copy.start()
         up_copies.append(copy)
+    attend(range(quarter))
     attend(range(quarter, 2 * quarter))
 
     base = [jnp.zeros((tokens, weight.shape[2]), jnp.float32) for _ in range(2)]
@@ -368,7 +383,27 @@
         factors = up_t[z]
         update = dot_nn(high, factors) + dot_nn(rest, factors)
         proj.append(base[z] + adapter_scale * update)
-    count = rows * per_row
+    for k in range(kv_here):
+        columns = slice(k * head_dim, (k + 1) * head_dim)
+        key = proj[0][:, columns]
+        new_acc[0, :, columns] = key * cos_k + pltpu.roll(key, half, 1) * sin_k
+    new_acc[1] = proj[1]
+    new_copy = pltpu.make_async_copy(new_acc, new_hbm, in_sem.at[5])
+    new_copy.start()
+    new_copy.wait()
+    for copy in out_copies:
+        copy.wait()
+    for copy in to_across + to_sibling + forward + up_copies + low_copies:
+        copy.wait_send()
+
+
+def new_token_kernel(new_ref, q_ref, out_ref, peak_ref, sum_ref, new_kv_ref, attended_ref):
+    rows, steps = attended_ref.shape[:2]
+    tokens = rows * steps
+    kv_here, count, head_dim = q_ref.shape
+    per_row = count // rows
+    group = per_row // steps
+    factor = math.log2(math.e) / math.sqrt(head_dim)
     row_at = lax.broadcasted_iota(jnp.int32, (count, tokens), 0)
     col_at = lax.broadcasted_iota(jnp.int32, (count, tokens), 1)
     seen = (row_at // per_row == col_at // steps) & (
@@ -376,20 +411,19 @@
     )
     for k in range(kv_here):
         columns = slice(k * head_dim, (k + 1) * head_dim)
-        key = proj[0][:, columns]
-        key = key * cos_k + pltpu.roll(key, half, 1) * sin_k
-        value = proj[1][:, columns]
+        key = new_ref[0, :, columns]
+        value = new_ref[1, :, columns]
         for r in range(rows):
             span = slice(r * steps, (r + 1) * steps)
             new_kv_ref[0, r, :, columns] = key[span].astype(jnp.bfloat16)
             new_kv_ref[1, r, :, columns] = value[span].astype(jnp.bfloat16)
-        scores = jnp.where(seen, dot_nt(q_rot[k], key.astype(jnp.bfloat16)), -1e30)
-        peak_old = peak_acc[k]
+        scores = jnp.where(seen, dot_nt(q_ref[k], key.astype(jnp.bfloat16)), -1e30)
+        peak_old = peak_ref[k]
         peak = jnp.maximum(peak_old, jnp.max(scores, axis=1, keepdims=True))
         expo = jnp.exp2((scores - peak[:, :tokens]) * factor)
         keep = jnp.exp2((peak_old - peak) * factor)
-        total = sum_acc[k] * keep + jnp.sum(expo, axis=1, keepdims=True)
-        output = out_acc[k] * keep + dot_nn(expo.astype(jnp.bfloat16), value.astype(jnp.bfloat16))
+        total = sum_ref[k] * keep + jnp.sum(expo, axis=1, keepdims=True)
+        output = out_ref[k] * keep + dot_nn(expo.astype(jnp.bfloat16), value.astype(jnp.bfloat16))
         output = output / total
         for r in range(rows):
             for g in range(group):
@@ -398,9 +432,6 @@
                 attended_ref[r, :, head * head_dim : (head + 1) * head_dim] = output[
                     at : at + steps
                 ].astype(jnp.bfloat16)
-
-    for copy in to_across + to_sibling + forward + up_copies + low_copies:
-        copy.wait_send()
 
 
 def on_device_kernel(hidden, queries, weight, down, up, cache, fill, tp):
@@ -413,14 +444,18 @@
     dma = pltpu.SemaphoreType.DMA
     f32, bf16 = jnp.float32, jnp.bfloat16
     moved = sum(math.prod(a.shape) * 2 for a in (hidden, weight, cache))
-    return pl.pallas_call(
+    held = (kv_here, rows * per_row, head_dim)
+    middle = pl.pallas_call(
         kernel,
         out_shape=(
-            jax.ShapeDtypeStruct((2, rows, steps, weight.shape[2]), bf16),
-            jax.ShapeDtypeStruct(queries.shape, bf16),
+            jax.ShapeDtypeStruct((2, tokens, weight.shape[2]), f32),
+            jax.ShapeDtypeStruct(held, bf16),
+            jax.ShapeDtypeStruct(held, f32),
+            jax.ShapeDtypeStruct(held, f32),
+            jax.ShapeDtypeStruct(held, f32),
         ),
         in_specs=[hbm_spec] * 7,
-        out_specs=(vmem_spec, vmem_spec),
+        out_specs=(hbm_spec,) * 5,
         scratch_shapes=[
             pltpu.SMEM(fill.shape, jnp.int32),
             pltpu.VMEM(hidden.shape, bf16),
@@ -434,11 +469,12 @@
             pltpu.VMEM(cache.shape[1:], bf16),
             pltpu.VMEM((rows * 2 * steps, head_dim), f32),
             pltpu.VMEM((rows * 2 * steps, head_dim), f32),
-            pltpu.VMEM((kv_here, rows * per_row, head_dim), bf16),
-            pltpu.VMEM((kv_here, rows * per_row, head_dim), f32),
-            pltpu.VMEM((kv_here, rows * per_row, head_dim), f32),
-            pltpu.VMEM((kv_here, rows * per_row, head_dim), f32),
-            dma((5,)),
+            pltpu.VMEM(held, bf16),
+            pltpu.VMEM(held, f32),
+            pltpu.VMEM(held, f32),
+            pltpu.VMEM(held, f32),
+            pltpu.VMEM((2, tokens, weight.shape[2]), f32),
+            dma((6,)),
             dma((2, W_CHUNKS)),
             dma((rows,)),
             dma((rows,)),
@@ -448,6 +484,7 @@
             dma((3,)),
             dma((tp - 1,)),
             dma((tp - 1,)),
+            dma((rows, 4)),
         ],
         compiler_params=pltpu.CompilerParams(
             collective_id=0, has_side_effects=True, vmem_limit_bytes=64 * 1024 * 1024
@@ -456,6 +493,16 @@
             flops=700_000_000, bytes_accessed=moved, transcendentals=800_000
         ),
     )(fill, hidden, queries, weight, down, jnp.swapaxes(up, 1, 2), cache)
+    return pl.pallas_call(
+        new_token_kernel,
+        out_shape=(
+            jax.ShapeDtypeStruct((2, rows, steps, weight.shape[2]), bf16),
+            jax.ShapeDtypeStruct(queries.shape, bf16),
+        ),
+        in_specs=[vmem_spec] * 5,
+        out_specs=(vmem_spec, vmem_spec),
+        compiler_params=pltpu.CompilerParams(vmem_limit_bytes=64 * 1024 * 1024),
+    )(*middle)
 
 
 def on_device(*args, mesh):

time: 25.4 us -> 23.7 us (0.933)
  local copies, waits for them, and re-layouts: 2.99 us -> 0 us
  Pallas kernels: 21.6 us -> 22.9 us
    unnamed x2 -> x0, local copies, waits for them, and re-layouts: 2.99 us -> none
    pallas_call x1 -> x2, Pallas kernels: 21.6 us -> 22.9 us  [the longest x1 20.4 us: on_device_kernel(): pl.pallas_call(kernel, out_shape=(jax.ShapeDtypeStruct((2, tokens, weight...]
where the time goes in v4:
time: 23.7 us; the launch traced here: 23.6 us
  Pallas kernels  22.9 us (97%)
  between operations  0.64 us (3%)
    pallas_call x1, Pallas kernels, on_device_kernel(): pl.pallas_call(kernel, out_shape=(jax.ShapeDtypeStruct((2, tokens, weight...  20.4 us
    pallas_call x1, Pallas kernels, on_device_kernel(): pl.pallas_call(new_token_kernel, out_shape=(jax.ShapeDtypeStruct((2, rows...  2.48 us

profile of v4, /device:TPU:0, one launch (start us, length us, event | category | flops | bytes accessed | tf_op | source)
XLA Modules:
  0.0 23.6 jit_solution(14798623291393848576)
XLA Ops:
  0.6 20.4 %shard_map.86 = (f32[2,32,256]{2,1,0:T(8,128)}, bf16[2,256,128]{2,1,0:T(8,128)(2,1)}, f32[2,256,128]{2,1,0:T(8,128)}, f32[2,256,128]{2,1,0:T(8,128)}, f32[2,256,128]{2,1,0:T(8,128)}) custom-call(s32[8]{0:T(128)} %fill_hbm.1, bf16[8,4,8192]{2,1,0:T(4,128)(2,1)} %hidden_hbm.1, bf16[8,4,2048]{2,1,0:T(4,128)(2,1)} %queries_hbm.1, ...), custom_call_target="tpu_custom_call" | custom-call | flops 700000000 | bytes 21495808 | tf_op jit(solution)/shard_map/pallas_call | solution.py:448
  21.1 2.5 %shard_map.87 = (bf16[2,8,4,256]{3,2,1,0:T(4,128)(2,1)}, bf16[8,4,2048]{2,1,0:T(4,128)(2,1)}) custom-call(f32[2,32,256]{2,1,0:T(8,128)} %get-tuple-element.7.new_ref, bf16[2,256,128]{2,1,0:T(8,128)(2,1)} %get-tuple-element.8.q_ref, f32[2,256,128]{2,1,0:T(8,128)} %get-tuple-element.9.out_ref, f32[2,256,128]{2,1,0:T(8,128)} %get-tuple-element.10.peak_ref, ...), custom_call_target="tpu_custom_call" | custom-call | tf_op jit(solution)/shard_map/pallas_call | solution.py:496

commit v5 on v4

--- a/solution.py
+++ b/solution.py
@@ -329,17 +329,15 @@
     attend(range(quarter))
     attend(range(quarter, 2 * quarter))
 
+    for z in range(2):
+        to_across[z].wait_recv()
+        forward[z].start()
     base = [jnp.zeros((tokens, weight.shape[2]), jnp.float32) for _ in range(2)]
     for c in range(W_CHUNKS):
         for z in range(2):
             weight_copies[c * 2 + z].wait()
             span = slice(c * depth, (c + 1) * depth)
             base[z] = base[z] + dot_nn(hidden_flat[:, span], weight[z, span, :])
-
-    for z in range(2):
-        to_across[z].wait_recv()
-        forward[z].start()
-    attend(range(2 * quarter, 3 * quarter))
 
     def low_of(slot):
         span = pl.ds(pl.multiple_of((owners[slot] * tp + t) * part, part), part)
@@ -364,6 +362,7 @@
         copy.start()
         low_copies.append(copy)
 
+    attend(range(2 * quarter, 3 * quarter))
     attend(range(3 * quarter, rows))
 
     for copy in low_copies:

time: 23.7 us -> 25.2 us (1.063)
  Pallas kernels: 22.9 us -> 24.4 us
    pallas_call x1, Pallas kernels: 20.4 us -> 21.9 us  [on_device_kernel(): pl.pallas_call(kernel, out_shape=(jax.ShapeDtypeStruct((2, tokens, weight...]
where the time goes in v5:
time: 25.2 us; the launch traced here: 25 us
  Pallas kernels  24.4 us (97%)
  between operations  0.64 us (3%)
    pallas_call x1, Pallas kernels, on_device_kernel(): pl.pallas_call(kernel, out_shape=(jax.ShapeDtypeStruct((2, tokens, weight...  21.9 us
    pallas_call x1, Pallas kernels, on_device_kernel(): pl.pallas_call(new_token_kernel, out_shape=(jax.ShapeDtypeStruct((2, rows...  2.48 us

profile of v5, /device:TPU:0, one launch (start us, length us, event | category | flops | bytes accessed | tf_op | source)
XLA Modules:
  0.0 25.0 jit_solution(6615285447844404563)
XLA Ops:
  0.6 21.9 %shard_map.86 = (f32[2,32,256]{2,1,0:T(8,128)}, bf16[2,256,128]{2,1,0:T(8,128)(2,1)}, f32[2,256,128]{2,1,0:T(8,128)}, f32[2,256,128]{2,1,0:T(8,128)}, f32[2,256,128]{2,1,0:T(8,128)}) custom-call(s32[8]{0:T(128)} %fill_hbm.1, bf16[8,4,8192]{2,1,0:T(4,128)(2,1)} %hidden_hbm.1, bf16[8,4,2048]{2,1,0:T(4,128)(2,1)} %queries_hbm.1, ...), custom_call_target="tpu_custom_call" | custom-call | flops 700000000 | bytes 21495808 | tf_op jit(solution)/shard_map/pallas_call | solution.py:447
  22.6 2.5 %shard_map.87 = (bf16[2,8,4,256]{3,2,1,0:T(4,128)(2,1)}, bf16[8,4,2048]{2,1,0:T(4,128)(2,1)}) custom-call(f32[2,32,256]{2,1,0:T(8,128)} %get-tuple-element.7.new_ref, bf16[2,256,128]{2,1,0:T(8,128)(2,1)} %get-tuple-element.8.q_ref, f32[2,256,128]{2,1,0:T(8,128)} %get-tuple-element.9.out_ref, f32[2,256,128]{2,1,0:T(8,128)} %get-tuple-element.10.peak_ref, ...), custom_call_target="tpu_custom_call" | custom-call | tf_op jit(solution)/shard_map/pallas_call | solution.py:495
